TPU v7x, 128 devices: a whole 4x4x4 slice. The times are simulated.
128 devices in a mesh: row: 8 (over y, x_lo), col: 16 (over x_hi, z, core).
Axes of the slice: x: 4 (x_hi: 2, x_lo: 2; x = x_hi * 2 + x_lo), y: 4, z: 4, core: 2. Of those that a mesh axis runs over, the one named last changes fastest.
Arguments:
- apanel: bfloat16 [32768, 16384], P('row', 'col'), may hold values from -6 to 6
- rowmask: int32 [256, 16], P('row', 'col'), may hold values from 0 to 1, as said below
- qpanel: bfloat16 [2, 8192, 16384], P(None, 'row', 'col'), may hold values from -0.109375 to 0.109375
Outputs:
- product: bfloat16 [32768, 16384], P('row', 'col')
Inputs may be any that keep to these rules, and one draw needn't show every extreme that they name: `rowmask`: write k = (i + j) mod 16 for column j of tile row i (rows i*32 to i*32 + 31). Tiles with k less than half of 16 have 1 to 24 entries equal to 1 in their column; the others 1 to 8. In every tile row the tile with k = 0 has exactly 24 and the tile with k equal to half of 16 exactly 8.
All inputs are finite; a program needn't handle non-finite values.
Results may differ from a plain program's by a relative error of at most 0.004.
Values may be sent and summed in bfloat16 or wider, within the bound.
A program may use at most 256 MiB of HBM per device.

v0:
```python
import jax
import jax.numpy as jnp
from jax import lax
from jax.sharding import PartitionSpec as P

BS = 128
LR = 32
LK = 8
LC = 8
SHIFTS = 3
MAXNZ = 24


def from_behind(x, axis, by):
    length = lax.axis_size(axis)
    return lax.ppermute(x, axis, [(i, (i + by) % length) for i in range(length)])


def compact_rows(band_tile, row_flags):
    ranked = jnp.argsort(1 - row_flags, stable=True)
    row_slots = ranked[:MAXNZ]
    is_kept = jnp.take(row_flags, row_slots) > 0
    blocks = band_tile.reshape(LR, BS, LK * BS)
    picked = jnp.take(blocks, row_slots, axis=0)
    picked = jnp.where(is_kept[:, None, None], picked, jnp.zeros((), picked.dtype))
    return (picked, row_slots)


def row_terms(picked, factor):
    return jnp.einsum("tpk,kq->tpq", picked, factor, preferred_element_type=jnp.float32)


def per_device(apanel, rowmask, qpanel):
    grid_rows = lax.axis_size("row")
    row_at = lax.axis_index("row")
    totals = jnp.zeros((LR, BS, LC * BS), jnp.float32)
    row_flags = rowmask.reshape(LR)
    band_tile = apanel
    qtiles = qpanel
    for offset in range(SHIFTS):
        picked, row_slots = compact_rows(band_tile, row_flags)
        current = qtiles[0]
        totals = totals.at[row_slots].add(row_terms(picked, current))
        if offset + 1 < SHIFTS:
            band_tile, row_flags = from_behind((band_tile, row_flags), "col", -1)
            arrived = from_behind(qtiles, "row", -1)
            qtiles = jnp.where(row_at == grid_rows - 1, arrived[::-1], arrived)
    return totals.reshape(LR * BS, LC * BS).astype(jnp.bfloat16)


def solution(mesh):
    in_specs = (P("row", "col"), P("row", "col"), P(None, "row", "col"))
    out_specs = P("row", "col")
    return jax.shard_map(
        per_device, mesh=mesh, in_specs=in_specs, out_specs=out_specs, check_vma=False
    )
```

profile of v0, /device:TPU:97, one launch (start us, length us, event | category | flops | bytes accessed | tf_op | source)
XLA Modules:
  0.0 477.6 jit_solution(17427532198760692696)
XLA Ops:
  0.0 0.7 collective-permute-start.1
  0.7 3.7 collective-permute-start.2
  4.3 137.2 %collective-permute-done.1 = bf16[4096,1024]{1,0:T(8,128)(2,1)} collective-permute-done((bf16[4096,1024]{1,0:T(8,128)(2,1)}, bf16[4096,1024]{1,0:T(8,128)(2,1)}, u32[]{:S(2)}, u32[]{:S(2)}) %collective-permute-start.1) | collective-permute-done | bytes 8388640 | tf_op jit(solution)/shard_map/ppermute | solution.py:16
  141.5 0.0 collective-permute-start.4
  141.5 0.0 collective-permute-start
  141.5 0.7 broadcast_subtract_fusion.2
  142.2 1.6 sort.45
  143.8 1.4 gather_fusion
  145.2 7.9 %gather_fusion.1 = bf16[24,128,1024]{2,1,0:T(8,128)(2,1)} fusion(bf16[32,128,1024]{2,1,0:T(8,128)(2,1)} %bitcast.20, s32[1024]{0:T(1024)S(1)} %pad_clamp_fusion.2), kind=kCustom, calls=%fused_computation.1.clone | custom fusion | bytes 12583008 | tf_op jit(solution)/shard_map/jit(_take)/gather | solution.py:24
  153.0 0.0 copy-start
  153.1 0.0 collective-permute-done.2
  153.1 7.8 %reverse_select_fusion = bf16[2,1024,1024]{2,1,0:T(8,128)(2,1)} fusion(bf16[2,1024,1024]{2,1,0:T(8,128)(2,1)} %collective-permute-done.2, pred[]{:T(512)S(6)} %eq.4), kind=kLoop, calls=%fused_computation.15 | loop fusion | flops 2097152 | bytes 8388609 | tf_op jit(solution)/shard_map/jit(_where)/select_n | solution.py:47
  160.9 0.0 collective-permute-start.5
  160.9 0.0 copy-done
  160.9 10.7 %fusion.2 = f32[24,128,1024]{2,1,0:T(8,128)} fusion(bf16[24,128,1024]{2,1,0:T(8,128)(2,1)S(1)} %copy-done, pred[24]{0:T(512)(128)(4,1)S(1)} %get-tuple-element.17, pred[24]{0:T(512)(128)(4,1)S(1)} %select_compare_fusion.2, bf16[2,1024,1024]{2,1,0:T(8,128)(2,1)} %param.9), kind=kOutput, calls=%fused_computation.14 | convolution fusion | flops 6448742400 | bytes 20971568 | tf_op jit(solution)/shard_map/tpk,kq->tpq/dot_general | solution.py:30
  171.6 7.9 %broadcast_in_dim.51 = f32[32,128,1024]{2,1,0:T(8,128)} broadcast(f32[]{:T(128)} %constant.24.clone.1), dimensions={} | broadcast | bytes 16777220 | tf_op jit(solution)/shard_map/broadcast_in_dim | solution.py:36
  179.4 27.3 %scatter_fusion = f32[32,128,1024]{2,1,0:T(8,128)} fusion(f32[32,128,1024]{2,1,0:T(8,128)} %broadcast_in_dim.51, s32[24]{0:T(128)S(1)} %get-tuple-element.18, f32[24,128,1024]{2,1,0:T(8,128)} %fusion.2), kind=kCustom, calls=%fused_computation.6 | custom fusion | flops 3145728 | bytes 37748832 | tf_op jit(solution)/shard_map/scatter-add | solution.py:43
  206.7 114.5 %collective-permute-done = s32[32]{0:T(128)S(1)} collective-permute-done((s32[32]{0:T(128)}, s32[32]{0:T(128)S(1)}, u32[]{:S(2)}, u32[]{:S(2)}) %collective-permute-start) | collective-permute-done | bytes 160 | tf_op jit(solution)/shard_map/ppermute | solution.py:16
  321.3 1.6 sort.46
  322.9 0.0 collective-permute-start.3
  322.9 0.7 gather_fusion.2
  323.6 42.5 %collective-permute-done.3 = s32[32]{0:T(128)S(1)} collective-permute-done((s32[32]{0:T(128)S(1)}, s32[32]{0:T(128)S(1)}, u32[]{:S(2)}, u32[]{:S(2)}) %collective-permute-start.3) | collective-permute-done | bytes 160 | tf_op jit(solution)/shard_map/ppermute | solution.py:16
  366.1 1.6 sort.47
  367.7 0.7 gather_fusion.4
  368.4 7.9 %gather_fusion.3 = bf16[24,128,1024]{2,1,0:T(8,128)(2,1)} fusion(bf16[32,128,1024]{2,1,0:T(8,128)(2,1)} %bitcast.4, s32[1024]{0:T(1024)S(1)} %pad_clamp_fusion.1), kind=kCustom, calls=%fused_computation.4.clone | custom fusion | bytes 12583008 | tf_op jit(solution)/shard_map/jit(_take)/gather | solution.py:24
  376.3 12.2 %fusion.1 = f32[24,128,1024]{2,1,0:T(8,128)} fusion(bf16[24,128,1024]{2,1,0:T(8,128)(2,1)} %gather_fusion.3, pred[24]{0:T(512)(128)(4,1)S(1)} %get-tuple-element.15, pred[24]{0:T(512)(128)(4,1)S(1)} %select_compare_fusion.1, bf16[2,1024,1024]{2,1,0:T(8,128)(2,1)} %reverse_select_fusion), kind=kOutput, calls=%fused_computation.12 | convolution fusion | flops 6448742400 | bytes 20971568 | tf_op jit(solution)/shard_map/tpk,kq->tpq/dot_general | solution.py:30
  388.5 27.3 %scatter_fusion.1 = f32[32,128,1024]{2,1,0:T(8,128)} fusion(f32[32,128,1024]{2,1,0:T(8,128)} %scatter_fusion, s32[24]{0:T(128)S(1)} %get-tuple-element.16, f32[24,128,1024]{2,1,0:T(8,128)} %fusion.1), kind=kCustom, calls=%fused_computation.7 | custom fusion | flops 3145728 | bytes 37748832 | tf_op jit(solution)/shard_map/scatter-add | solution.py:43
  415.9 0.0 collective-permute-done.5
  415.9 4.7 rev.7
  420.5 0.0 collective-permute-done.4
  420.5 7.9 %gather_fusion.5 = bf16[24,128,1024]{2,1,0:T(8,128)(2,1)} fusion(bf16[32,128,1024]{2,1,0:T(8,128)(2,1)} %bitcast.7, s32[1024]{0:T(1024)S(1)} %pad_clamp_fusion), kind=kCustom, calls=%fused_computation.5.clone | custom fusion | bytes 12583008 | tf_op jit(solution)/shard_map/jit(_take)/gather | solution.py:24
  428.4 12.8 %fusion = f32[24,128,1024]{2,1,0:T(8,128)} fusion(bf16[24,128,1024]{2,1,0:T(8,128)(2,1)} %gather_fusion.5, pred[24]{0:T(512)(128)(4,1)S(1)} %get-tuple-element.13, pred[24]{0:T(512)(128)(4,1)S(1)} %select_compare_fusion, bf16[2,1024,1024]{2,1,0:T(8,128)(2,1)} %collective-permute-done.5, bf16[2,1024,1024]{2,1,0:T(8,128)(2,1)} %rev.7, pred[]{:T(512)S(6)} %eq.4), kind=kOutput, calls=%fused_computation.10 | convolution fusion | flops 6449790976 | bytes 23068720 | tf_op jit(solution)/shard_map/tpk,kq->tpq/dot_general | solution.py:30
  441.2 27.3 %scatter_fusion.2 = f32[32,128,1024]{2,1,0:T(8,128)} fusion(f32[32,128,1024]{2,1,0:T(8,128)} %scatter_fusion.1, s32[24]{0:T(128)S(1)} %get-tuple-element.14, f32[24,128,1024]{2,1,0:T(8,128)} %fusion), kind=kCustom, calls=%fused_computation.8 | custom fusion | flops 3145728 | bytes 37748832 | tf_op jit(solution)/shard_map/scatter-add | solution.py:43
  468.5 9.1 %convert_element_type.6 = bf16[32,128,1024]{2,1,0:T(8,128)(2,1)} convert(f32[32,128,1024]{2,1,0:T(8,128)} %scatter_fusion.2) | non-fusion elementwise | flops 4194304 | bytes 25165824 | tf_op jit(solution)/shard_map/convert_element_type | solution.py:48
  (14 shorter events, 0.1 us)
Async XLA Ops:
  0.0 141.5 %collective-permute-start.1 = (bf16[4096,1024]{1,0:T(8,128)(2,1)}, bf16[4096,1024]{1,0:T(8,128)(2,1)}, u32[]{:S(2)}, u32[]{:S(2)}) collective-permute-start(bf16[4096,1024]{1,0:T(8,128)(2,1)} %param.7), channel_id=1, source_target_pairs={{0,15},{1,0},{2,1},{3,2},{4,3},{5,4},{6,5},{7,6},{8,7},{9,8},{10,9... | collective-permute-start | bytes 25165832 | tf_op jit(solution)/shard_map/ppermute | solution.py:16
  0.7 152.4 %collective-permute-start.2 = (bf16[2,1024,1024]{2,1,0:T(8,128)(2,1)}, bf16[2,1024,1024]{2,1,0:T(8,128)(2,1)}, u32[]{:S(2)}, u32[]{:S(2)}) collective-permute-start(bf16[2,1024,1024]{2,1,0:T(8,128)(2,1)} %param.9), channel_id=1, source_target_pairs={{0,112},{16,0},{32,16},{48,32},{64,48},{80,64},{96,80},{112,96},{1... | collective-permute-start | bytes 12582920 | tf_op jit(solution)/shard_map/ppermute | solution.py:16
  141.5 279.0 %collective-permute-start.4 = (bf16[4096,1024]{1,0:T(8,128)(2,1)}, bf16[4096,1024]{1,0:T(8,128)(2,1)}, u32[]{:S(2)}, u32[]{:S(2)}) collective-permute-start(bf16[4096,1024]{1,0:T(8,128)(2,1)} %collective-permute-done.1), channel_id=1, source_target_pairs={{0,15},{1,0},{2,1},{3,2},{4,3},{5,4},{6,5},{7,6},{8,7},{9,8},{10,9... | collective-permute-start | bytes 25165832 | tf_op jit(solution)/shard_map/ppermute | solution.py:16
  141.5 179.8 %collective-permute-start = (s32[32]{0:T(128)}, s32[32]{0:T(128)S(1)}, u32[]{:S(2)}, u32[]{:S(2)}) collective-permute-start(s32[32]{0:T(128)} %bitcast.18), channel_id=1, source_target_pairs={{0,15},{1,0},{2,1},{3,2},{4,3},{5,4},{6,5},{7,6},{8,7},{9,8},{10,9... | collective-permute-start | bytes 392 | tf_op jit(solution)/shard_map/ppermute | solution.py:16
  153.0 7.8 %copy-start = (bf16[24,128,1024]{2,1,0:T(8,128)(2,1)S(1)}, bf16[24,128,1024]{2,1,0:T(8,128)(2,1)}, u32[]{:S(2)}) copy-start(bf16[24,128,1024]{2,1,0:T(8,128)(2,1)} %gather_fusion.1) | copy-start | bytes 18874372
  160.9 255.0 %collective-permute-start.5 = (bf16[2,1024,1024]{2,1,0:T(8,128)(2,1)}, bf16[2,1024,1024]{2,1,0:T(8,128)(2,1)}, u32[]{:S(2)}, u32[]{:S(2)}) collective-permute-start(bf16[2,1024,1024]{2,1,0:T(8,128)(2,1)} %reverse_select_fusion), channel_id=1, source_target_pairs={{0,112},{16,0},{32,16},{48,32},{64,48},{80,64},{96,80},{112,96},{1... | collective-permute-start | bytes 12582920 | tf_op jit(solution)/shard_map/ppermute | solution.py:16
  322.9 43.2 %collective-permute-start.3 = (s32[32]{0:T(128)S(1)}, s32[32]{0:T(128)S(1)}, u32[]{:S(2)}, u32[]{:S(2)}) collective-permute-start(s32[32]{0:T(128)S(1)} %collective-permute-done), channel_id=1, source_target_pairs={{0,15},{1,0},{2,1},{3,2},{4,3},{5,4},{6,5},{7,6},{8,7},{9,8},{10,9... | collective-permute-start | bytes 392 | tf_op jit(solution)/shard_map/ppermute | solution.py:16
where the time goes:
time: 478 us
  waiting for transfers between devices  294 us (62%)
  other arithmetic  104 us (22%)
  local copies, waits for them, and re-layouts  38.9 us (8%)
  matrix products  35.8 us (7%)
    ppermute x6, waiting for transfers between devices, from_behind(): lax.ppermute(x, axis, [(i, (i + by) % length) for i in range(length)])  294 us
    scatter-add x3, other arithmetic, per_device(): totals = totals.at[row_slots].add(row_terms(picked, current))  81.9 us
    dot_general x3, matrix products, row_terms(): jnp.einsum('tpk,kq->tpq', picked, factor, preferred_element_type=jnp.floa...  35.8 us
    gather x3, local copies, waits for them, and re-layouts, compact_rows(): picked = jnp.take(blocks, row_slots, axis=0)  23.6 us
  transfers between devices with their start and end apart: 6, of which 3 were waited for; matrix products, arithmetic and copies ran while one was open for 26% of the time, Pallas kernels for 0%

commit v1 on v0

v1 whole, which is shorter than its diff:
```python
import jax
import jax.numpy as jnp
from jax import lax
from jax.experimental import pallas as pl
from jax.experimental.pallas import tpu as pltpu
from jax.sharding import PartitionSpec as P

BS = 128
LR = 32
WIDTH = 1024
MAXNZ = 24
LIGHTNZ = 8
PANELS = 16
GRID_ROWS = 8
GROUP = 4
GROUPS = MAXNZ // GROUP
QPARTS = WIDTH // BS
MESH = pl.DeviceIdType.MESH

OUT = [
    [
        262, 262, 518, 518, 12550, 12550, 8, 8, 8962, 8962, 8708, 8708, 0, 0, 0, 0,
        4614, 4614, 4710, 4710, 4102, 4102, 8866, 8866, 12834, 12834, 0, 0, 0, 0, 12360, 0,
        1286, 1286, 1544, 1544, 1028, 1028, 0, 0, 9986, 9986, 0, 0, 0, 0, 9223, 9223,
        5382, 5382, 5734, 5734, 0, 9508, 0, 0, 14082, 14082, 0, 0, 13378, 13378, 13414, 13414,
        2566, 2566, 2661, 2661, 2049, 2049, 0, 0, 10754, 10754, 0, 0, 6405, 6405, 10326, 10326,
        6726, 6726, 6818, 6818, 0, 0, 0, 0, 14882, 14882, 10792, 14914, 2311, 2311, 14393, 14393,
        3590, 3590, 0, 0, 3074, 3074, 0, 0, 12034, 12034, 11784, 11784, 7430, 7430, 11270, 11270,
        7752, 12072, 0, 0, 0, 0, 0, 0, 3364, 15880, 3108, 3108, 3430, 3430, 3686, 3686,
    ],
    [
        774, 774, 12292, 12292, 8452, 8452, 12802, 12802, 0, 0, 0, 0, 0, 0, 0, 0,
        4870, 4870, 8196, 8196, 8258, 8258, 0, 0, 0, 0, 0, 0, 0, 0, 0, 0,
        1798, 1798, 13922, 13922, 13316, 13316, 0, 0, 0, 0, 0, 0, 0, 0, 5123, 5123,
        5638, 5638, 9732, 9732, 0, 0, 0, 0, 0, 0, 0, 0, 0, 0, 1668, 1668,
        2822, 2822, 14339, 14339, 0, 0, 0, 0, 0, 0, 0, 0, 10245, 10245, 6660, 6660,
        6918, 6918, 0, 0, 0, 0, 0, 0, 0, 0, 0, 0, 2066, 2066, 2737, 2737,
        3846, 3846, 0, 0, 0, 0, 0, 0, 0, 0, 7170, 7170, 3330, 3330, 7684, 7684,
        7944, 0, 0, 0, 0, 0, 0, 0, 15876, 3364, 15940, 16004, 15364, 15364, 15428, 15428,
    ],
    [
        13062, 13062, 0, 0, 0, 0, 0, 0, 0, 0, 0, 0, 0, 0, 0, 0,
        8774, 8774, 0, 0, 8514, 8514, 0, 0, 0, 0, 0, 0, 0, 0, 0, 0,
        13830, 13830, 0, 0, 9474, 9474, 0, 0, 0, 0, 0, 0, 0, 0, 0, 0,
        5894, 5894, 0, 0, 0, 0, 0, 0, 0, 0, 0, 0, 0, 0, 0, 0,
        15110, 15110, 14850, 14850, 0, 0, 0, 0, 0, 0, 0, 0, 0, 0, 0, 0,
        11014, 11014, 0, 0, 0, 0, 0, 0, 0, 0, 0, 0, 6481, 6481, 0, 0,
        16134, 16134, 0, 0, 0, 0, 0, 0, 0, 0, 0, 0, 7202, 7202, 0, 0,
        0, 0, 0, 0, 0, 0, 0, 0, 0, 0, 3938, 3938, 0, 0, 0, 0,
    ],
]
IN = [
    [
        1032, 1032, 17926, 17926, 6, 6, 18022, 18022, 8292, 8292, 612, 612, 16388, 16388, 1538, 1538,
        8710, 8710, 0, 0, 26118, 26118, 26214, 26214, 100, 100, 518, 518, 1154, 1154, 18118, 18118,
        2564, 2564, 19974, 19974, 2056, 2056, 20070, 20070, 19463, 19463, 2690, 2690, 10340, 10340, 3586, 3586,
        19571, 19571, 28166, 28166, 28262, 28262, 28358, 28358, 2628, 2628, 0, 0, 20166, 20166, 11778, 11778,
        4609, 4609, 29191, 29191, 22022, 22022, 22118, 22118, 21077, 21077, 0, 0, 5634, 5634, 30406, 30406,
        0, 0, 20997, 20997, 21604, 21604, 30310, 30310, 4179, 4179, 0, 0, 4226, 4226, 22214, 22214,
        6658, 6658, 23138, 23138, 24070, 24070, 24166, 24166, 23558, 23558, 0, 0, 22536, 22536, 7682, 7682,
        22658, 22658, 23046, 23046, 23652, 23652, 32392, 0, 31332, 31332, 0, 0, 15940, 15880, 24262, 24262,
    ],
    [
        0, 0, 0, 0, 0, 0, 0, 0, 8802, 8802, 8834, 8834, 26310, 26310, 0, 0,
        0, 0, 0, 0, 8198, 8198, 0, 0, 25608, 0, 0, 0, 9730, 9730, 0, 0,
        0, 0, 0, 0, 27748, 27748, 0, 0, 0, 0, 0, 10756, 0, 0, 0, 0,
        0, 0, 0, 0, 10246, 10246, 0, 0, 27138, 27138, 0, 0, 2178, 2178, 0, 0,
        29298, 29298, 0, 0, 4101, 4101, 0, 0, 21510, 21510, 0, 0, 28680, 0, 0, 0,
        0, 0, 29329, 29329, 30214, 30214, 0, 0, 29705, 29705, 0, 0, 13826, 13826, 0, 0,
        30724, 30724, 15876, 16004, 31750, 31750, 30850, 30850, 0, 0, 0, 0, 0, 0, 0, 32264,
        23170, 23170, 0, 0, 32264, 0, 0, 0, 31844, 31844, 0, 0, 30788, 30788, 0, 0,
    ],
    [
        0, 0, 0, 0, 0, 0, 0, 0, 0, 0, 0, 0, 9218, 9218, 0, 0,
        0, 0, 0, 0, 0, 0, 0, 0, 0, 0, 0, 0, 0, 0, 0, 0,
        0, 0, 0, 0, 0, 0, 0, 0, 0, 0, 0, 0, 0, 0, 0, 0,
        0, 0, 0, 0, 0, 0, 0, 0, 27654, 27654, 0, 0, 0, 0, 0, 0,
        0, 0, 0, 0, 29841, 29841, 0, 0, 0, 0, 0, 0, 0, 0, 0, 0,
        0, 0, 0, 0, 12290, 12290, 0, 0, 0, 0, 0, 0, 0, 28674, 0, 0,
        0, 0, 31238, 31238, 0, 0, 0, 0, 0, 0, 0, 0, 0, 0, 0, 0,
        0, 0, 0, 0, 0, 0, 0, 0, 0, 0, 0, 0, 0, 0, 0, 0,
    ],
]
SLOTS = 12


def pick(values, at):
    bit = 1
    while len(values) > 1:
        odd = (at // bit) % 2 == 1
        values = [
            a if isinstance(a, int) and isinstance(b, int) and a == b else jnp.where(odd, b, a)
            for a, b in zip(values[::2], values[1::2])
        ]
        bit *= 2
    return jnp.int32(values[0]) if isinstance(values[0], int) else values[0]


def on_chip(chip, core):
    x, y, z = chip // 16, (chip // 4) % 4, chip % 4
    return {"row": y * 2 + x % 2, "col": (x // 2) * 8 + z * 2 + core}


def chunks_of(row, col):
    return jnp.where((row + col) % PANELS < PANELS // 2, MAXNZ, LIGHTNZ)


def kernel(
    band, flags, qtiles, product, raw, tiles, relay, factors, parts, flags1, flags2, ranks, following, slots,
    load_sem, own_send, pair_send, relay_send, q_send, q_fwd, flag_send, got1, got2, relay_got, q_got1, q_got2, flag_got, out_sem,
):
    row, col = lax.axis_index("row"), lax.axis_index("col")
    core = col % 2
    odd_row = row % 2
    back1, back2 = (col + PANELS - 1) % PANELS, (col + PANELS - 2) % PANELS
    ahead1, ahead2 = (col + 1) % PANELS, (col + 2) % PANELS
    pair = {"row": row, "col": col + 1 - 2 * core}
    behind = {"row": row, "col": back2}
    row_behind, row_ahead = (row + GRID_ROWS - 2) % GRID_ROWS, (row + 2) % GRID_ROWS
    row_pair = {"row": row + 1 - 2 * odd_row, "col": col}
    n0, n1, n2 = chunks_of(row, col), chunks_of(row, ahead1), chunks_of(row, ahead2)

    load_raw = pltpu.make_async_copy(band, raw, load_sem.at[0])
    load_raw.start()
    load_q = pltpu.make_async_copy(qtiles.at[0], factors.at[0], load_sem.at[1])
    load_q.start()

    me = row * PANELS + col
    outs = []
    first = 0
    for table in OUT:
        code = pick(table, me)
        outs.append((code // 256, (code // 16) % 16, first, code % 16))
        first = first + code % 16
    straight = first
    ins = []
    slot = 0
    for table in IN:
        code = pick(table, me)
        ins.append((code // 512, (code // 16) % 32, slot, code % 16))
        slot = slot + code % 16

    barrier = pltpu.get_barrier_semaphore()

    def greet(device):
        pl.semaphore_signal(barrier, inc=1, device_id=device, device_id_type=MESH)

    for device in ({"row": row, "col": ahead1}, {"row": row, "col": ahead2}, pair, {"row": row_ahead, "col": col}, row_pair):
        greet(device)
    expected = 5
    for chip, _, _, count in outs:
        expected = expected + jnp.where(count > 0, 1, 0)
    for chip, _, _, count in ins:
        expected = expected + jnp.where(count > 0, 1, 0)
        target = on_chip(chip, core)

        @pl.when(count > 0)
        def _():
            greet({"row": target["row"], "col": (target["col"] + 2) % PANELS})

    for table in OUT:
        code = pick(table, row * PANELS + ahead2)

        @pl.when(code > 0)
        def _():
            greet(on_chip(code // 256, core))

    following[LR] = LR - 1

    @pl.loop(0, LR)
    def _(t):
        r = LR - 1 - t
        following[r] = jnp.where(flags[r] > 0, r, following[r + 1])

    @pl.loop(0, MAXNZ)
    def _(t):
        before = jnp.where(t == 0, -1, slots[jnp.maximum(t - 1, 0)])
        slots[t] = following[before + 1]

    def remote(src, dst, send, recv, device):
        return pltpu.make_async_remote_copy(
            src_ref=src, dst_ref=dst, send_sem=send, recv_sem=recv, device_id=device, device_id_type=MESH
        )

    def landed(dst, sem):
        pltpu.make_async_copy(dst, dst, sem).wait()

    pl.semaphore_wait(barrier, expected)

    wrapped = jnp.where(row < 2, 1, 0)

    def q_rows(u):
        return pl.ds(u * BS if isinstance(u, int) else pl.multiple_of(u * BS, BS), BS)

    def q_copy(u):
        return remote(
            qtiles.at[wrapped, q_rows(u)], factors.at[2, q_rows(u)], q_send.at[u], q_got2.at[u], {"row": row_behind, "col": col}
        )

    def q_pair_own(u):
        return remote(qtiles.at[0, q_rows(u)], factors.at[1, q_rows(u)], q_fwd.at[u], q_got1.at[u], row_pair)

    def q_pair_forward(u):
        return remote(factors.at[2, q_rows(u)], factors.at[1, q_rows(u)], q_fwd.at[u], q_got1.at[u], row_pair)

    flag_copies = [
        remote(flags, flags1, flag_send.at[0], flag_got.at[0], {"row": row, "col": back1}),
        remote(flags, flags2, flag_send.at[1], flag_got.at[1], behind),
    ]
    for copy in flag_copies:
        copy.start()

    @pl.loop(0, QPARTS)
    def _(u):
        q_copy(u).start()

        @pl.when(odd_row == 1)
        def _():
            q_pair_own(u).start()

    load_raw.wait()

    @pl.loop(0, MAXNZ)
    def _(t):
        @pl.when(t < n0)
        def _():
            tiles[0, t] = raw[slots[t]]

    def own_copy(t):
        return remote(tiles.at[0, t], tiles.at[2, t], own_send.at[t], got2.at[t], behind)

    def own_to_relay(t, chip, at):
        return remote(tiles.at[0, t], relay.at[at], own_send.at[t], relay_got.at[at], on_chip(chip, core))

    def own_to_pair(t):
        return remote(tiles.at[0, t], tiles.at[1, t], pair_send.at[t], got1.at[t], pair)

    def forward_to_pair(t):
        return remote(tiles.at[2, t], tiles.at[1, t], pair_send.at[t], got1.at[t], pair)

    def pass_on(at, chip, t):
        return remote(relay.at[at], tiles.at[2, t], relay_send.at[at], got2.at[t], on_chip(chip, core))

    @pl.loop(0, MAXNZ)
    def _(u):
        for chip, at, t, count in outs:
            @pl.when(u < count)
            def _():
                own_to_relay(t + u, chip, at + u).start()

        @pl.when(u < n0 - straight)
        def _():
            own_copy(straight + u).start()

    @pl.when(core == 1)
    def _():
        @pl.loop(0, n0)
        def _(t):
            own_to_pair(t).start()

    load_q.wait()

    def multiply(s, v):
        lhs = tiles[s, pl.ds(v * GROUP, GROUP)].reshape(GROUP * BS, WIDTH)
        out = jnp.dot(lhs, factors[s], preferred_element_type=jnp.float32)
        parts[s, pl.ds(v * GROUP, GROUP)] = out.astype(jnp.bfloat16).reshape(GROUP, BS, WIDTH)

    @pl.loop(0, GROUPS)
    def _(v):
        @pl.loop(v * GROUP, (v + 1) * GROUP)
        def _(u):
            @pl.when((odd_row == 0) & (u < QPARTS))
            def _():
                landed(factors.at[2, q_rows(u)], q_got2.at[u])
                q_pair_forward(u).start()

            for chip, t, at, count in ins:
                @pl.when(u < count)
                def _():
                    landed(relay.at[at + u], relay_got.at[at + u])
                    pass_on(at + u, chip, t + u).start()

        @pl.when(v * GROUP < n0)
        def _():
            multiply(0, v)

    @pl.loop(0, QPARTS)
    def _(u):
        landed(factors.at[1, q_rows(u)], q_got1.at[u])

        @pl.when(odd_row == 1)
        def _():
            landed(factors.at[2, q_rows(u)], q_got2.at[u])

    def take1(v):
        @pl.loop(v * GROUP, (v + 1) * GROUP)
        def _(u):
            landed(tiles.at[1, u], got1.at[u])

        multiply(1, v)

    @pl.loop(0, GROUPS)
    def _(v):
        @pl.when((core == 0) & (v * GROUP < n1))
        def _():
            take1(v)

        @pl.when(v * GROUP < n2)
        def _():
            @pl.loop(v * GROUP, (v + 1) * GROUP)
            def _(u):
                landed(tiles.at[2, u], got2.at[u])

                @pl.when(core == 0)
                def _():
                    forward_to_pair(u).start()

            multiply(2, v)

        @pl.when((core == 1) & (v * GROUP < n1))
        def _():
            take1(v)

    for copy in flag_copies:
        copy.wait()
    for s, (held, n) in enumerate(((flags, n0), (flags1, n1), (flags2, n2))):
        def place(r, count):
            ranks[s, r] = jnp.minimum(count, n - 1)
            return count + held[r]

        lax.fori_loop(0, LR, place, jnp.int32(0))

    @pl.loop(0, LR)
    def _(r):
        there = [held[r] > 0 for held in (flags, flags1, flags2)]
        at = [ranks[s, r] for s in range(3)]

        @pl.loop(0, BS, step=16)
        def _(h):
            lines = pl.ds(pl.multiple_of(h, 16), 16)
            total = jnp.zeros((16, WIDTH), jnp.float32)
            for s in range(3):
                total += jnp.where(there[s], parts[s, at[s], lines].astype(jnp.float32), 0.0)
            raw[r, lines] = total.astype(jnp.bfloat16)

        pltpu.make_async_copy(raw.at[r], product.at[r], out_sem.at[0]).start()

    @pl.loop(0, QPARTS)
    def _(u):
        q_copy(u).wait_send()

        @pl.when(odd_row == 1)
        def _():
            q_pair_own(u).wait_send()

        @pl.when(odd_row == 0)
        def _():
            q_pair_forward(u).wait_send()

    @pl.loop(0, n0)
    def _(t):
        own_copy(t).wait_send()

    @pl.loop(0, jnp.where(core == 0, n2, n0))
    def _(t):
        own_to_pair(t).wait_send()

    @pl.loop(0, slot)
    def _(at):
        pass_on(at, 0, 0).wait_send()

    pltpu.make_async_copy(raw, product, out_sem.at[0]).wait()


def per_device(apanel, rowmask, qpanel):
    dma = pltpu.SemaphoreType.DMA
    whole = pl.BlockSpec(memory_space=pl.ANY)
    product = pl.pallas_call(
        kernel,
        out_shape=jax.ShapeDtypeStruct((LR, BS, WIDTH), jnp.bfloat16),
        in_specs=[whole, pl.BlockSpec(memory_space=pltpu.SMEM), whole],
        out_specs=whole,
        scratch_shapes=[
            pltpu.VMEM((LR, BS, WIDTH), jnp.bfloat16),
            pltpu.VMEM((3, MAXNZ, BS, WIDTH), jnp.bfloat16),
            pltpu.VMEM((SLOTS, BS, WIDTH), jnp.bfloat16),
            pltpu.VMEM((3, WIDTH, WIDTH), jnp.bfloat16),
            pltpu.VMEM((3, MAXNZ, BS, WIDTH), jnp.bfloat16),
            pltpu.SMEM((LR,), jnp.int32),
            pltpu.SMEM((LR,), jnp.int32),
            pltpu.SMEM((3, LR), jnp.int32),
            pltpu.SMEM((LR + 1,), jnp.int32),
            pltpu.SMEM((LR,), jnp.int32),
            dma((2,)),
            dma((MAXNZ,)),
            dma((MAXNZ,)),
            dma((SLOTS,)),
            dma((QPARTS,)),
            dma((QPARTS,)),
            dma((2,)),
            dma((MAXNZ,)),
            dma((MAXNZ,)),
            dma((SLOTS,)),
            dma((QPARTS,)),
            dma((QPARTS,)),
            dma((2,)),
            dma((1,)),
        ],
        compiler_params=pltpu.CompilerParams(collective_id=0, has_side_effects=True, vmem_limit_bytes=60 << 20),
    )(apanel.reshape(LR, BS, WIDTH), rowmask.reshape(LR), qpanel)
    return product.reshape(LR * BS, WIDTH)


def solution(mesh):
    in_specs = (P("row", "col"), P("row", "col"), P(None, "row", "col"))
    return jax.shard_map(per_device, mesh=mesh, in_specs=in_specs, out_specs=P("row", "col"), check_vma=False)
```

time: 478 us -> 164 us (0.34)
  the two profiles are of different devices: /device:TPU:97 before, /device:TPU:123 now
where the time goes in v1:
time: 164 us; the launch traced here: 163 us
  Pallas kernels  156 us (95%)
  local copies, waits for them, and re-layouts  7.76 us (5%)
    pallas_call x1, Pallas kernels, per_device(): pl.pallas_call(kernel, out_shape=jax.ShapeDtypeStruct((LR, BS, WIDTH), jn...  156 us
    unnamed x1, local copies, waits for them, and re-layouts  7.76 us

profile of v1, /device:TPU:123, one launch (start us, length us, event | category | flops | bytes accessed | tf_op | source)
XLA Modules:
  0.0 163.4 jit_solution(16873382376012817404)
XLA Ops:
  0.0 155.7 %shard_map.37 = bf16[32,128,1024]{2,1,0:T(8,128)(2,1)} custom-call(bf16[32,128,1024]{2,1,0:T(8,128)(2,1)} %bitcast.4, s32[32]{0:T(128)} %bitcast.5, bf16[2,1024,1024]{2,1,0:T(8,128)(2,1)} %qtiles.1), custom_call_target="tpu_custom_call" | custom-call | tf_op jit(solution)/shard_map/pallas_call | solution.py:378
  155.7 7.8 %copy.5 = bf16[4096,1024]{1,0:T(8,128)(2,1)} copy(bf16[4096,1024]{1,0:T(8,128)(2,1)} %bitcast.3) | data formatting | bytes 16777216

commit v2 on v1

v2 whole, which is shorter than its diff:
```python
import jax
import jax.numpy as jnp
from jax import lax
from jax.experimental import pallas as pl
from jax.experimental.pallas import tpu as pltpu
from jax.sharding import PartitionSpec as P

BS = 128
LR = 32
WIDTH = 1024
MAXNZ = 24
LIGHTNZ = 8
PANELS = 16
GRID_ROWS = 8
GROUP = 4
GROUPS = MAXNZ // GROUP
QPARTS = WIDTH // BS
MESH = pl.DeviceIdType.MESH

OUT = [
    [
        518, 518, 12806, 12806, 5, 5, 1540, 1540, 4865, 4865, 0, 0, 0, 0, 0, 0,
        4614, 4614, 7174, 7174, 4102, 4102, 5634, 0, 13137, 13137, 0, 0, 0, 0, 12322, 0,
        1798, 1798, 13318, 13318, 1030, 1030, 0, 0, 9729, 9729, 0, 0, 0, 0, 9222, 9222,
        5894, 5894, 9318, 9318, 5122, 0, 0, 0, 13825, 13825, 0, 0, 9474, 0, 13414, 13414,
        2822, 2822, 2596, 2596, 0, 0, 0, 0, 11009, 11009, 0, 0, 9509, 9477, 6741, 6741,
        6918, 6918, 0, 6818, 0, 0, 0, 0, 15105, 15105, 0, 13842, 2405, 2405, 2662, 2662,
        3638, 3638, 0, 0, 0, 0, 0, 0, 8017, 8017, 8198, 8198, 7430, 7430, 11270, 11270,
        12044, 0, 0, 0, 0, 0, 0, 0, 0, 16140, 12374, 12342, 12550, 12550, 15366, 15366,
    ],
    [
        774, 774, 3075, 3075, 3332, 3332, 3587, 3587, 0, 0, 0, 0, 0, 0, 0, 0,
        8966, 8966, 8707, 8707, 8451, 8451, 0, 0, 0, 0, 0, 0, 0, 0, 0, 0,
        14086, 14086, 2562, 2562, 6402, 6402, 0, 0, 0, 0, 0, 0, 0, 0, 8755, 8755,
        9990, 9990, 6659, 6659, 0, 0, 0, 0, 0, 0, 0, 0, 0, 0, 1698, 1698,
        14854, 14854, 3123, 3123, 0, 0, 0, 0, 0, 0, 0, 0, 6434, 6434, 10276, 10276,
        10758, 10758, 0, 0, 0, 0, 0, 0, 0, 0, 0, 0, 14339, 14339, 14387, 14387,
        3846, 3846, 0, 0, 0, 0, 0, 0, 0, 0, 10338, 10338, 8499, 8499, 8803, 8803,
        7686, 0, 0, 0, 0, 0, 0, 0, 0, 15878, 15875, 15971, 3394, 3394, 3731, 3731,
    ],
    [
        13061, 13061, 0, 0, 0, 0, 12290, 12290, 0, 0, 0, 0, 0, 0, 0, 0,
        4885, 4885, 0, 0, 0, 0, 0, 0, 0, 0, 0, 0, 0, 0, 0, 0,
        1605, 1605, 1681, 1681, 2305, 2305, 0, 0, 0, 0, 0, 0, 0, 0, 0, 0,
        5669, 5637, 0, 0, 0, 0, 0, 0, 0, 0, 0, 0, 0, 0, 12353, 12321,
        2325, 2325, 6706, 6706, 0, 0, 0, 0, 0, 0, 0, 0, 10242, 10242, 0, 0,
        7941, 7941, 0, 0, 0, 0, 0, 0, 0, 0, 0, 0, 6465, 6465, 0, 0,
        15125, 15125, 0, 0, 0, 0, 0, 0, 0, 0, 11777, 11777, 0, 0, 0, 0,
        0, 0, 0, 0, 0, 0, 0, 0, 0, 0, 0, 0, 3169, 3169, 0, 0,
    ],
]
IN = [
    [
        821, 821, 0, 0, 18214, 18214, 18118, 18118, 22822, 22822, 8947, 8947, 8435, 8435, 26310, 26310,
        8998, 8998, 0, 0, 26406, 26406, 1649, 1649, 1266, 1266, 31526, 31526, 294, 294, 18037, 18037,
        2854, 2854, 0, 0, 1348, 1348, 20262, 20262, 19750, 19750, 27234, 21301, 3697, 3697, 28358, 28358,
        11106, 0, 0, 0, 9570, 28277, 28454, 28454, 2342, 2342, 0, 0, 11889, 11889, 20166, 20166,
        0, 0, 2801, 2801, 2306, 2306, 22310, 22310, 21234, 21234, 0, 0, 30406, 30406, 5745, 5745,
        0, 0, 2818, 2818, 10483, 10483, 30502, 30502, 29443, 29443, 0, 0, 22214, 22214, 13937, 13937,
        243, 243, 756, 756, 1299, 1299, 24262, 24262, 23846, 23846, 0, 0, 22769, 22769, 32460, 0,
        8486, 8486, 23334, 23334, 32358, 0, 30325, 30325, 32038, 32038, 0, 0, 30963, 15974, 0, 16076,
    ],
    [
        0, 0, 0, 0, 0, 0, 0, 0, 0, 0, 23283, 23283, 19699, 19699, 0, 0,
        0, 0, 0, 0, 0, 0, 26229, 26229, 25698, 27889, 0, 0, 0, 0, 9841, 9841,
        0, 0, 0, 0, 20085, 20085, 0, 0, 10534, 10534, 21301, 0, 0, 0, 0, 0,
        0, 0, 0, 0, 28277, 0, 0, 0, 27942, 27942, 0, 0, 0, 29026, 0, 0,
        0, 0, 22133, 22133, 4420, 4420, 0, 0, 21748, 21748, 0, 0, 0, 0, 0, 0,
        0, 0, 21266, 21266, 4338, 4338, 0, 0, 29939, 29939, 0, 0, 0, 0, 24181, 24181,
        4371, 4371, 31490, 31490, 24358, 24358, 0, 0, 0, 0, 0, 0, 0, 0, 0, 0,
        0, 0, 0, 0, 0, 0, 7793, 7793, 0, 0, 0, 0, 0, 30963, 0, 0,
    ],
    [
        0, 0, 0, 0, 0, 0, 0, 0, 0, 0, 0, 0, 23795, 23795, 0, 0,
        0, 0, 0, 0, 0, 0, 0, 0, 27889, 31014, 0, 0, 0, 0, 0, 0,
        0, 0, 0, 0, 2289, 2289, 0, 0, 0, 0, 0, 0, 0, 0, 0, 0,
        0, 0, 0, 0, 0, 0, 0, 0, 0, 0, 0, 0, 0, 0, 0, 0,
        0, 0, 29493, 29493, 29990, 29990, 0, 0, 22786, 22786, 0, 0, 0, 0, 0, 0,
        0, 0, 29425, 29425, 21813, 21813, 0, 0, 0, 0, 0, 0, 0, 0, 0, 0,
        31473, 31473, 0, 0, 31987, 31987, 0, 0, 0, 0, 0, 0, 0, 0, 0, 0,
        0, 0, 0, 0, 0, 0, 0, 0, 0, 0, 0, 0, 0, 0, 0, 0,
    ],
    [
        0, 0, 0, 0, 0, 0, 0, 0, 0, 0, 0, 0, 0, 0, 0, 0,
        0, 0, 0, 0, 0, 0, 0, 0, 31014, 0, 0, 0, 0, 0, 0, 0,
        0, 0, 0, 0, 27906, 27906, 0, 0, 0, 0, 0, 0, 0, 0, 0, 0,
        0, 0, 0, 0, 0, 0, 0, 0, 0, 0, 0, 0, 0, 0, 0, 0,
        0, 0, 0, 0, 0, 0, 0, 0, 0, 0, 0, 0, 0, 0, 0, 0,
        0, 0, 0, 0, 0, 12386, 0, 0, 0, 0, 0, 0, 0, 0, 0, 0,
        0, 0, 0, 0, 0, 0, 0, 0, 0, 0, 0, 0, 0, 0, 0, 0,
        0, 0, 0, 0, 0, 0, 0, 0, 0, 0, 0, 0, 0, 0, 0, 0,
    ],
]
SLOTS = 12

TICKS = 12
Q_TICKS = 8
RELAY_TICKS = 8
STRAIGHT_TICKS = 10
LAG = 1
STRAIGHT_LAG = 2
TICK2 = Q_TICKS + LAG
TICK1 = TICK2 + LAG + 1


def pick(values, at):
    bit = 1
    while len(values) > 1:
        odd = (at // bit) % 2 == 1
        values = [
            a if isinstance(a, int) and isinstance(b, int) and a == b else jnp.where(odd, b, a)
            for a, b in zip(values[::2], values[1::2])
        ]
        bit *= 2
    return jnp.int32(values[0]) if isinstance(values[0], int) else values[0]


def on_chip(chip, core):
    x, y, z = chip // 16, (chip // 4) % 4, chip % 4
    return {"row": y * 2 + x % 2, "col": (x // 2) * 8 + z * 2 + core}


def chunks_of(row, col):
    return jnp.where((row + col) % PANELS < PANELS // 2, MAXNZ, LIGHTNZ)


def kernel(
    band, flags, qtiles, packed, others, raw, tiles, relay, factors, parts, flags1, flags2, following, slots,
    load_sem, own_send, pair_send, relay_send, q_send, q_fwd, flag_send, got1, got2, relay_got, q_got1, q_got2, flag_got, out_sem,
):
    row, col = lax.axis_index("row"), lax.axis_index("col")
    core = col % 2
    odd_row = row % 2
    back1, back2 = (col + PANELS - 1) % PANELS, (col + PANELS - 2) % PANELS
    ahead1, ahead2 = (col + 1) % PANELS, (col + 2) % PANELS
    pair = {"row": row, "col": col + 1 - 2 * core}
    behind = {"row": row, "col": back2}
    row_behind, row_ahead = (row + GRID_ROWS - 2) % GRID_ROWS, (row + 2) % GRID_ROWS
    row_pair = {"row": row + 1 - 2 * odd_row, "col": col}
    n0, n1, n2 = chunks_of(row, col), chunks_of(row, ahead1), chunks_of(row, ahead2)

    load_raw = pltpu.make_async_copy(band, raw, load_sem.at[0])
    load_raw.start()
    load_q = pltpu.make_async_copy(qtiles.at[0], factors.at[0], load_sem.at[1])
    load_q.start()

    me = row * PANELS + col
    outs = []
    first = n0
    for table in OUT:
        code = pick(table, me)
        first = first - code % 16
        outs.append((code // 256, (code // 16) % 16, first, code % 16))
    relayed = n0 - first
    ins = []
    slot = 0
    for table in IN:
        code = pick(table, me)
        ins.append((code // 512, (code // 16) % 32, slot, code % 16))
        slot = slot + code % 16

    barrier = pltpu.get_barrier_semaphore()

    def greet(device):
        pl.semaphore_signal(barrier, inc=1, device_id=device, device_id_type=MESH)

    for device in ({"row": row, "col": ahead1}, {"row": row, "col": ahead2}, pair, {"row": row_ahead, "col": col}, row_pair):
        greet(device)
    expected = 5
    for chip, _, _, count in outs:
        expected = expected + jnp.where(count > 0, 1, 0)
    for chip, _, _, count in ins:
        expected = expected + jnp.where(count > 0, 1, 0)
        target = on_chip(chip, core)

        @pl.when(count > 0)
        def _():
            greet({"row": target["row"], "col": (target["col"] + 2) % PANELS})

    relayed_in, relayed_in1 = jnp.int32(0), jnp.int32(0)
    for table in OUT:
        relayed_in1 = relayed_in1 + pick(table, row * PANELS + ahead1) % 16
        code = pick(table, row * PANELS + ahead2)
        relayed_in = relayed_in + code % 16

        @pl.when(code > 0)
        def _():
            greet(on_chip(code // 256, core))

    following[LR] = LR - 1

    @pl.loop(0, LR)
    def _(t):
        r = LR - 1 - t
        following[r] = jnp.where(flags[r] > 0, r, following[r + 1])

    @pl.loop(0, MAXNZ)
    def _(t):
        before = jnp.where(t == 0, -1, slots[jnp.maximum(t - 1, 0)])
        slots[t] = following[before + 1]

    def remote(src, dst, send, recv, device):
        return pltpu.make_async_remote_copy(
            src_ref=src, dst_ref=dst, send_sem=send, recv_sem=recv, device_id=device, device_id_type=MESH
        )

    def landed(dst, sem):
        pltpu.make_async_copy(dst, dst, sem).wait()

    pl.semaphore_wait(barrier, expected)

    wrapped = jnp.where(row < 2, 1, 0)

    def q_rows(u):
        return pl.ds(u * BS if isinstance(u, int) else pl.multiple_of(u * BS, BS), BS)

    def q_copy(u):
        return remote(
            qtiles.at[wrapped, q_rows(u)], factors.at[2, q_rows(u)], q_send.at[u], q_got2.at[u], {"row": row_behind, "col": col}
        )

    def q_pair_own(u):
        return remote(qtiles.at[0, q_rows(u)], factors.at[1, q_rows(u)], q_fwd.at[u], q_got1.at[u], row_pair)

    def q_pair_forward(u):
        return remote(factors.at[2, q_rows(u)], factors.at[1, q_rows(u)], q_fwd.at[u], q_got1.at[u], row_pair)

    flag_copies = [
        remote(flags, flags1, flag_send.at[0], flag_got.at[0], {"row": row, "col": back1}),
        remote(flags, flags2, flag_send.at[1], flag_got.at[1], behind),
    ]
    for copy in flag_copies:
        copy.start()

    load_raw.wait()

    @pl.loop(0, MAXNZ)
    def _(t):
        @pl.when(t < n0)
        def _():
            tiles[0, t] = raw[slots[t]]

    def own_copy(t):
        return remote(tiles.at[0, t], tiles.at[2, t], own_send.at[t], got2.at[t], behind)

    def own_to_relay(t, chip, at):
        return remote(tiles.at[0, t], relay.at[at], own_send.at[t], relay_got.at[at], on_chip(chip, core))

    def own_to_pair(t):
        return remote(tiles.at[0, t], tiles.at[1, t], pair_send.at[t], got1.at[t], pair)

    def forward_to_pair(t):
        return remote(tiles.at[2, t], tiles.at[1, t], pair_send.at[t], got1.at[t], pair)

    def pass_on(at, chip, t):
        return remote(relay.at[at], tiles.at[2, t], relay_send.at[at], got2.at[t], on_chip(chip, core))

    @pl.when(core == 1)
    def _():
        @pl.loop(0, n0)
        def _(t):
            own_to_pair(t).start()

    load_q.wait()

    def put_away(s, v):
        group = pl.ds(v * GROUP, GROUP)
        return pltpu.make_async_copy(parts.at[s, group], packed.at[s, group], out_sem.at[s, v])

    def multiply(s, v):
        lhs = tiles[s, pl.ds(v * GROUP, GROUP)].reshape(GROUP * BS, WIDTH)
        out = jnp.dot(lhs, factors[s], preferred_element_type=jnp.float32)
        parts[s, pl.ds(v * GROUP, GROUP)] = out.astype(jnp.bfloat16).reshape(GROUP, BS, WIDTH)
        put_away(s, v).start()

    def due(count, tick, ticks):
        return jnp.clip((count * (tick + 1) + ticks - 1) // ticks, 0, count)

    def multiply1(v):
        @pl.loop(v * GROUP, (v + 1) * GROUP)
        def _(u):
            landed(tiles.at[1, u], got1.at[u])

        multiply(1, v)

    def take2(u):
        landed(tiles.at[2, u], got2.at[u])

        @pl.when(core == 0)
        def _():
            forward_to_pair(u).start()

    straight_in = n2 - relayed_in

    def ready2(tick):
        there = due(straight_in, tick - STRAIGHT_LAG, STRAIGHT_TICKS) // GROUP
        return jnp.where(tick < TICK2, 0, there)

    def ready1(tick):
        there = due(n1 - relayed_in1, tick - STRAIGHT_LAG - 1, STRAIGHT_TICKS) // GROUP
        there = jnp.where(core == 0, jnp.minimum(n1 // GROUP, tick - TICK1 + 1), there)
        return jnp.where(tick < TICK1, 0, there)

    @pl.loop(0, TICKS)
    def _(tick):
        @pl.loop(due(QPARTS, tick - 1, Q_TICKS), due(QPARTS, tick, Q_TICKS))
        def _(u):
            q_copy(u).start()

            @pl.when(odd_row == 1)
            def _():
                q_pair_own(u).start()

        for chip, at, t, count in outs:
            @pl.loop(due(count, tick - 1, RELAY_TICKS), due(count, tick, RELAY_TICKS))
            def _(u):
                own_to_relay(t + u, chip, at + u).start()

        @pl.loop(due(n0 - relayed, tick - 1, STRAIGHT_TICKS), due(n0 - relayed, tick, STRAIGHT_TICKS))
        def _(u):
            own_copy(u).start()

        @pl.when((tick % 2 == 1) & (tick < 2 * GROUPS) & (tick // 2 * GROUP < n0))
        def _():
            multiply(0, tick // 2)

        then = tick - LAG

        @pl.when(odd_row == 0)
        def _():
            @pl.loop(due(QPARTS, then - 1, Q_TICKS), due(QPARTS, then, Q_TICKS))
            def _(u):
                landed(factors.at[2, q_rows(u)], q_got2.at[u])
                q_pair_forward(u).start()

        for chip, t, at, count in ins:
            @pl.loop(due(count, then - 1, RELAY_TICKS), due(count, then, RELAY_TICKS))
            def _(u):
                landed(relay.at[at + u], relay_got.at[at + u])
                pass_on(at + u, chip, t + u).start()

        then2 = tick - STRAIGHT_LAG

        @pl.loop(due(straight_in, then2 - 1, STRAIGHT_TICKS), due(straight_in, then2, STRAIGHT_TICKS))
        def _(u):
            take2(u)

        @pl.when((odd_row == 1) & (tick == TICK2))
        def _():
            @pl.loop(0, QPARTS)
            def _(u):
                landed(factors.at[2, q_rows(u)], q_got2.at[u])

        @pl.when(tick == TICK1)
        def _():
            @pl.loop(0, QPARTS)
            def _(u):
                landed(factors.at[1, q_rows(u)], q_got1.at[u])

        @pl.loop(ready2(tick - 1), ready2(tick))
        def _(v):
            multiply(2, v)

        @pl.loop(ready1(tick - 1), ready1(tick))
        def _(v):
            multiply1(v)

    @pl.loop(straight_in, n2)
    def _(u):
        take2(u)

    @pl.loop(ready2(TICKS - 1), n2 // GROUP)
    def _(v):
        multiply(2, v)

    @pl.loop(ready1(TICKS - 1), n1 // GROUP)
    def _(v):
        multiply1(v)

    for copy in flag_copies:
        copy.wait()

    @pl.loop(0, LR)
    def _(r):
        others[0, r] = flags1[r]
        others[1, r] = flags2[r]

    @pl.loop(0, QPARTS)
    def _(u):
        q_copy(u).wait_send()

        @pl.when(odd_row == 1)
        def _():
            q_pair_own(u).wait_send()

        @pl.when(odd_row == 0)
        def _():
            q_pair_forward(u).wait_send()

    @pl.loop(0, n0)
    def _(t):
        own_copy(t).wait_send()

    @pl.loop(0, jnp.where(core == 0, n2, n0))
    def _(t):
        own_to_pair(t).wait_send()

    @pl.loop(0, slot)
    def _(at):
        pass_on(at, 0, 0).wait_send()

    for s, n in enumerate((n0, n1, n2)):
        @pl.loop(0, n // GROUP)
        def _(v):
            put_away(s, v).wait()


def combine(flags, others, packed, product, parts, rows, got, out_sem):
    row, col = lax.axis_index("row"), lax.axis_index("col")
    groups = [chunks_of(row, (col + s) % PANELS) // GROUP for s in range(3)]

    def fetch(s, v):
        group = pl.ds(v * GROUP, GROUP)
        return pltpu.make_async_copy(packed.at[s, group], parts.at[s, group], got.at[s, v])

    def put(r):
        return pltpu.make_async_copy(rows.at[r], product.at[r], out_sem.at[r])

    @pl.loop(0, GROUPS)
    def _(v):
        for s in range(3):
            @pl.when(v < groups[s])
            def _():
                fetch(s, v).start()

    def batch(b, counts):
        for s in range(3):
            @pl.when(b < groups[s])
            def _():
                fetch(s, b).wait()

        for t in range(GROUP):
            r = b * GROUP + t
            there = [flags[r] > 0, others[0, r] > 0, others[1, r] > 0]
            counts = tuple(count + jnp.where(held, 1, 0) for count, held in zip(counts, there))
            at = [jnp.clip(count - 1, 0, MAXNZ - 1) for count in counts]

            @pl.loop(0, BS, step=16)
            def _(h):
                lines = pl.ds(pl.multiple_of(h, 16), 16)
                total = jnp.zeros((16, WIDTH), jnp.float32)
                for s in range(3):
                    total += jnp.where(there[s], parts[s, at[s], lines].astype(jnp.float32), 0.0)
                rows[r, lines] = total.astype(jnp.bfloat16)

            put(r).start()
        return counts

    lax.fori_loop(0, LR // GROUP, batch, (jnp.int32(0),) * 3)

    @pl.loop(0, LR)
    def _(r):
        put(r).wait()


def per_device(apanel, rowmask, qpanel):
    dma = pltpu.SemaphoreType.DMA
    whole = pl.BlockSpec(memory_space=pl.ANY)
    row_flags = rowmask.reshape(LR)
    scalars = pl.BlockSpec(memory_space=pltpu.SMEM)
    packed, others = pl.pallas_call(
        kernel,
        out_shape=(
            jax.ShapeDtypeStruct((3, MAXNZ, BS, WIDTH), jnp.bfloat16),
            jax.ShapeDtypeStruct((2, LR), jnp.int32),
        ),
        in_specs=[whole, scalars, whole],
        out_specs=(whole, scalars),
        scratch_shapes=[
            pltpu.VMEM((LR, BS, WIDTH), jnp.bfloat16),
            pltpu.VMEM((3, MAXNZ, BS, WIDTH), jnp.bfloat16),
            pltpu.VMEM((SLOTS, BS, WIDTH), jnp.bfloat16),
            pltpu.VMEM((3, WIDTH, WIDTH), jnp.bfloat16),
            pltpu.VMEM((3, MAXNZ, BS, WIDTH), jnp.bfloat16),
            pltpu.SMEM((LR,), jnp.int32),
            pltpu.SMEM((LR,), jnp.int32),
            pltpu.SMEM((LR + 1,), jnp.int32),
            pltpu.SMEM((LR,), jnp.int32),
            dma((2,)),
            dma((MAXNZ,)),
            dma((MAXNZ,)),
            dma((SLOTS,)),
            dma((QPARTS,)),
            dma((QPARTS,)),
            dma((2,)),
            dma((MAXNZ,)),
            dma((MAXNZ,)),
            dma((SLOTS,)),
            dma((QPARTS,)),
            dma((QPARTS,)),
            dma((2,)),
            dma((3, GROUPS)),
        ],
        compiler_params=pltpu.CompilerParams(collective_id=0, has_side_effects=True, vmem_limit_bytes=60 << 20),
    )(apanel.reshape(LR, BS, WIDTH), row_flags, qpanel)
    product = pl.pallas_call(
        combine,
        out_shape=jax.ShapeDtypeStruct((LR, BS, WIDTH), jnp.bfloat16),
        in_specs=[scalars, scalars, whole],
        out_specs=whole,
        scratch_shapes=[
            pltpu.VMEM((3, MAXNZ, BS, WIDTH), jnp.bfloat16),
            pltpu.VMEM((LR, BS, WIDTH), jnp.bfloat16),
            dma((3, GROUPS)),
            dma((LR,)),
        ],
        compiler_params=pltpu.CompilerParams(vmem_limit_bytes=60 << 20),
    )(row_flags, others, packed)
    return product.reshape(LR * BS, WIDTH)


def solution(mesh):
    in_specs = (P("row", "col"), P("row", "col"), P(None, "row", "col"))
    return jax.shard_map(per_device, mesh=mesh, in_specs=in_specs, out_specs=P("row", "col"), check_vma=False)
```

time: 164 us -> 132 us (0.80)
  the two profiles are of different devices: /device:TPU:123 before, /device:TPU:124 now
where the time goes in v2:
time: 132 us; the launch traced here: 131 us
  Pallas kernels  131 us (99%)
    pallas_call x1, Pallas kernels, per_device(): pl.pallas_call(kernel, out_shape=(jax.ShapeDtypeStruct((3, MAXNZ, BS, WID...  119 us
    pallas_call x1, Pallas kernels, per_device(): pl.pallas_call(combine, out_shape=jax.ShapeDtypeStruct((LR, BS, WIDTH), j...  12.3 us

profile of v2, /device:TPU:124, one launch (start us, length us, event | category | flops | bytes accessed | tf_op | source)
XLA Modules:
  0.0 131.4 jit_solution(17701439574034405781)
XLA Ops:
  0.0 119.1 %shard_map.37 = (bf16[3,24,128,1024]{3,2,1,0:T(8,128)(2,1)}, s32[2,32]{1,0:T(2,128)}) custom-call(bf16[32,128,1024]{2,1,0:T(8,128)(2,1)} %bitcast.3, s32[32]{0:T(128)} %bitcast.4, bf16[2,1024,1024]{2,1,0:T(8,128)(2,1)} %qtiles.1), custom_call_target="tpu_custom_call" | custom-call | tf_op jit(solution)/shard_map/pallas_call | solution.py:471
  119.1 12.3 %shard_map.38 = bf16[32,128,1024]{2,1,0:T(8,128)(2,1)} custom-call(s32[32]{0:T(128)} %bitcast.5, s32[2,32]{1,0:T(2,128)} %get-tuple-element.7.others, bf16[3,24,128,1024]{3,2,1,0:T(8,128)(2,1)} %get-tuple-element.8.packed), custom_call_target="tpu_custom_call" | custom-call | tf_op jit(solution)/shard_map/pallas_call | solution.py:506

commit v3 on v2

--- a/solution.py
+++ b/solution.py
@@ -433,6 +433,11 @@
             def _():
                 fetch(s, v).start()
 
+    @pl.loop(0, BS, step=16)
+    def _(h):
+        for s in range(3):
+            parts[s, MAXNZ, pl.ds(pl.multiple_of(h, 16), 16)] = jnp.zeros((16, WIDTH), jnp.bfloat16)
+
     def batch(b, counts):
         for s in range(3):
             @pl.when(b < groups[s])
@@ -443,15 +448,13 @@
             r = b * GROUP + t
             there = [flags[r] > 0, others[0, r] > 0, others[1, r] > 0]
             counts = tuple(count + jnp.where(held, 1, 0) for count, held in zip(counts, there))
-            at = [jnp.clip(count - 1, 0, MAXNZ - 1) for count in counts]
-
-            @pl.loop(0, BS, step=16)
+            at = [jnp.where(held, jnp.clip(count - 1, 0, MAXNZ - 1), MAXNZ) for count, held in zip(counts, there)]
+
+            @pl.loop(0, BS, step=16, unroll=4)
             def _(h):
                 lines = pl.ds(pl.multiple_of(h, 16), 16)
-                total = jnp.zeros((16, WIDTH), jnp.float32)
-                for s in range(3):
-                    total += jnp.where(there[s], parts[s, at[s], lines].astype(jnp.float32), 0.0)
-                rows[r, lines] = total.astype(jnp.bfloat16)
+                terms = [parts[s, at[s], lines].astype(jnp.float32) for s in range(3)]
+                rows[r, lines] = (terms[0] + terms[1] + terms[2]).astype(jnp.bfloat16)
 
             put(r).start()
         return counts
@@ -509,7 +512,7 @@
         in_specs=[scalars, scalars, whole],
         out_specs=whole,
         scratch_shapes=[
-            pltpu.VMEM((3, MAXNZ, BS, WIDTH), jnp.bfloat16),
+            pltpu.VMEM((3, MAXNZ + 1, BS, WIDTH), jnp.bfloat16),
             pltpu.VMEM((LR, BS, WIDTH), jnp.bfloat16),
             dma((3, GROUPS)),
             dma((LR,)),

time: 132 us -> 130 us (0.985)
  no operation moved by 1% of the time
where the time goes in v3:
time: 130 us
  Pallas kernels  130 us (100%)
    pallas_call x1, Pallas kernels, per_device(): pl.pallas_call(kernel, out_shape=(jax.ShapeDtypeStruct((3, MAXNZ, BS, WID...  119 us
    pallas_call x1, Pallas kernels, per_device(): pl.pallas_call(combine, out_shape=jax.ShapeDtypeStruct((LR, BS, WIDTH), j...  11.2 us

profile of v3, /device:TPU:124, one launch (start us, length us, event | category | flops | bytes accessed | tf_op | source)
XLA Modules:
  0.0 130.3 jit_solution(3162307682114000281)
XLA Ops:
  0.0 119.1 %shard_map.37 = (bf16[3,24,128,1024]{3,2,1,0:T(8,128)(2,1)}, s32[2,32]{1,0:T(2,128)}) custom-call(bf16[32,128,1024]{2,1,0:T(8,128)(2,1)} %bitcast.3, s32[32]{0:T(128)} %bitcast.4, bf16[2,1024,1024]{2,1,0:T(8,128)(2,1)} %qtiles.1), custom_call_target="tpu_custom_call" | custom-call | tf_op jit(solution)/shard_map/pallas_call | solution.py:474
  119.1 11.2 %shard_map.38 = bf16[32,128,1024]{2,1,0:T(8,128)(2,1)} custom-call(s32[32]{0:T(128)} %bitcast.5, s32[2,32]{1,0:T(2,128)} %get-tuple-element.7.others, bf16[3,24,128,1024]{3,2,1,0:T(8,128)(2,1)} %get-tuple-element.8.packed), custom_call_target="tpu_custom_call" | custom-call | tf_op jit(solution)/shard_map/pallas_call | solution.py:509
